TPU v7x, 32 devices: a whole 2x2x4 slice. The times are simulated.
32 devices in a mesh: fsdp: 16 (over z, x, core), dp: 2 (over y).
Axes of the slice: x: 2, y: 2, z: 4, core: 2. Of those that a mesh axis runs over, the one named last changes fastest.
Arguments:
- tokens: bfloat16 [16384, 1024], P(('fsdp', 'dp')), may hold values from -6 to 6
- encoder: bfloat16 [16384, 1024], P(('fsdp', 'dp')), may hold values from -6 to 6
- cotangent: bfloat16 [16384, 1024], P(('fsdp', 'dp')), may hold values from -6 to 6
- self_qkv: bfloat16 [3, 1024, 1024], P(None, 'fsdp'), may hold values from -0.1875 to 0.1875
- self_out: bfloat16 [1024, 1024], P('fsdp'), may hold values from -0.75 to 0.75
- cross_qkv: bfloat16 [3, 1024, 1024], P(None, 'fsdp'), may hold values from -0.1875 to 0.1875
- cross_out: bfloat16 [1024, 1024], P('fsdp'), may hold values from -0.75 to 0.75
- ffn_in: bfloat16 [1024, 4096], P('fsdp'), may hold values from -0.1875 to 0.1875
- ffn_out: bfloat16 [4096, 1024], P('fsdp'), may hold values from -0.09375 to 0.09375
- adapt_down: bfloat16 [1024, 512], replicated, may hold values from -0.1875 to 0.1875
- down_bias: float32 [512], replicated, may hold values from -2 to 2
- adapt_up: bfloat16 [512, 1024], replicated, may hold values from -0.25 to 0.25
- up_bias: float32 [1024], replicated, may hold values from -2 to 2
- norm_gain: float32 [3, 1024], replicated, may hold values from 0.25 to 1.75
- norm_bias: float32 [3, 1024], replicated, may hold values from -2 to 2
- bucket_shift: int32 [32], P(('fsdp', 'dp')), may hold values from 0 to 2, as said below
- seq_lengths: int32 [32, 4], P(('fsdp', 'dp')), may hold values from 64 to 512, as said below
- enc_lengths: int32 [32, 4], P(('fsdp', 'dp')), may hold values from 64 to 512, as said below
Outputs:
- output: bfloat16 [16384, 1024], P(('fsdp', 'dp'))
- grad_tokens: bfloat16 [16384, 1024], P(('fsdp', 'dp'))
- grad_encoder: bfloat16 [16384, 1024], P(('fsdp', 'dp'))
- grad_adapt_down: float32 [1024, 512], replicated
- grad_down_bias: float32 [512], replicated
- grad_adapt_up: float32 [512, 1024], replicated
- grad_up_bias: float32 [1024], replicated
- grad_norm_gain: float32 [3, 1024], replicated
- grad_norm_bias: float32 [3, 1024], replicated
Inputs may be any that keep to these rules, and one draw needn't show every extreme that they name: Some group has bucket_shift 0 and some group has 2; group g holds 4 >> bucket_shift[g] sequences. `seq_lengths`: entry j of a group is the valid length of its j-th sequence for j < 4 >> bucket_shift[g], and lies between half the bucket and the bucket; later entries are unused; in every group one sequence fills its bucket. `enc_lengths`: entry j of a group is the valid encoder length of its j-th sequence for j < 4 >> bucket_shift[g], and lies between half the bucket and the bucket; later entries are unused; in every group one sequence fills its bucket.
All inputs are finite; a program needn't handle non-finite values.
Results may differ from a plain program's by a relative error of at most 0.02.
Values may be sent and summed in bfloat16 or wider, within the bound.
A program may use at most 256 MiB of HBM per device.

v0:
```python
import jax
import jax.numpy as jnp
from jax import lax
from jax.sharding import PartitionSpec as P

HEADS = 16
STEP = 12


epsilon = 1e-05
ramp_steps = 4.0
masked_score = -1e30


def gelu_exact(values_in):
    return jax.nn.gelu(values_in, approximate=False)


def layer_stats(values_in):
    average = jnp.mean(values_in, -1, keepdims=True)
    centred = values_in - average
    inverse = lax.rsqrt(jnp.mean(centred * centred, -1, keepdims=True) + epsilon)
    return (centred * inverse, inverse)


def norm_back(grad_out, normal, inverse, norm_scale):
    grad_normal = grad_out * norm_scale
    grad_in = inverse * (
        grad_normal
        - jnp.mean(grad_normal, -1, keepdims=True)
        - normal * jnp.mean(grad_normal * normal, -1, keepdims=True)
    )
    return (grad_in, jnp.sum(grad_out * normal, 0), jnp.sum(grad_out, 0))


def mask_maker(bucket_code, seq_lens, rows_here, causal):
    bucket = rows_here // 4 * jnp.where(bucket_code == 0, 1, jnp.where(bucket_code == 1, 2, 4))
    key_pos = jnp.arange(rows_here, dtype=jnp.int32)
    key_seq = key_pos // bucket
    key_place = key_pos - key_seq * bucket
    slot_ids = jnp.arange(4, dtype=jnp.int32)
    key_len = jnp.sum(jnp.where(key_seq[:, None] == slot_ids[None, :], seq_lens[None, :], 0), 1)

    def mask_of(offset, block_rows):
        query_pos = offset + jnp.arange(block_rows, dtype=jnp.int32)
        query_seq = query_pos // bucket
        query_place = query_pos - query_seq * bucket
        allowed = (query_seq[:, None] == key_seq[None, :]) & (key_place[None, :] < key_len[None, :])
        if causal:
            allowed = allowed & (key_place[None, :] <= query_place[:, None])
        return allowed

    return mask_of


def split_heads(values_in):
    return values_in.reshape(values_in.shape[0], HEADS, -1)


def attend_forward(query_rows, key_rows, value_rows, mask_of):
    rows_here = query_rows.shape[0]
    block_rows = min(rows_here, 512)
    query_heads = split_heads(query_rows)
    key_heads = split_heads(key_rows)
    value_heads = split_heads(value_rows)
    scaling = query_heads.shape[-1] ** (-0.5)

    def one_block(offset):
        scores = (
            jnp.einsum("thd,shd->hts", query_heads, key_heads, preferred_element_type=jnp.float32)
            * scaling
        )
        scores = jnp.where(mask_of(offset, block_rows)[None], scores, masked_score)
        row_peak = jnp.max(scores, -1, keepdims=True)
        expanded = jnp.exp(scores - row_peak)
        row_total = jnp.sum(expanded, -1, keepdims=True)
        attn_probs = (expanded / row_total).astype(jnp.bfloat16)
        attended = jnp.einsum(
            "hts,shd->thd", attn_probs, value_heads, preferred_element_type=jnp.float32
        )
        return (attended.reshape(block_rows, -1), (row_peak + jnp.log(row_total))[..., 0])

    offsets = jnp.arange(rows_here // block_rows, dtype=jnp.int32) * block_rows
    attended, log_totals = lax.map(one_block, offsets)
    return (attended.reshape(rows_here, -1), log_totals)


def attend_backward(query_rows, key_rows, value_rows, grad_rows, log_totals, mask_of):
    rows_here = query_rows.shape[0]
    block_rows = min(rows_here, 512)
    query_heads = split_heads(query_rows)
    key_heads = split_heads(key_rows)
    value_heads = split_heads(value_rows)
    grad_heads = split_heads(grad_rows)
    scaling = query_heads.shape[-1] ** (-0.5)

    def one_block(running, item):
        offset, block_totals = item
        scores = (
            jnp.einsum("thd,shd->hts", query_heads, key_heads, preferred_element_type=jnp.float32)
            * scaling
        )
        scores = jnp.where(mask_of(offset, block_rows)[None], scores, masked_score)
        attn_probs = jnp.exp(scores - block_totals[..., None])
        grad_probs = jnp.einsum(
            "thd,shd->hts", grad_heads, value_heads, preferred_element_type=jnp.float32
        )
        row_delta = jnp.sum(attn_probs * grad_probs, -1, keepdims=True)
        grad_scores = (attn_probs * (grad_probs - row_delta)).astype(jnp.bfloat16)
        grad_query = (
            jnp.einsum("hts,shd->thd", grad_scores, key_heads, preferred_element_type=jnp.float32)
            * scaling
        )
        grad_keys = (
            running[0]
            + jnp.einsum(
                "hts,thd->shd", grad_scores, query_heads, preferred_element_type=jnp.float32
            )
            * scaling
        )
        grad_values = running[1] + jnp.einsum(
            "hts,thd->shd",
            attn_probs.astype(jnp.bfloat16),
            grad_heads,
            preferred_element_type=jnp.float32,
        )
        return ((grad_keys, grad_values), grad_query.reshape(block_rows, -1))

    offsets = jnp.arange(rows_here // block_rows, dtype=jnp.int32) * block_rows
    zeros_kd = jnp.zeros(key_heads.shape, jnp.float32)
    (grad_keys, grad_values), grad_query = lax.scan(
        one_block, (zeros_kd, zeros_kd), (offsets, log_totals)
    )
    return (
        grad_query.reshape(rows_here, -1).astype(jnp.bfloat16),
        grad_keys.reshape(key_rows.shape[0], -1).astype(jnp.bfloat16),
        grad_values.reshape(value_rows.shape[0], -1).astype(jnp.bfloat16),
    )


def local(
    tokens,
    encoder,
    cotangent,
    self_qkv,
    self_out,
    cross_qkv,
    cross_out,
    ffn_in,
    ffn_out,
    adapt_down,
    down_bias,
    adapt_up,
    up_bias,
    norm_gain,
    norm_bias,
    bucket_shift,
    seq_lengths,
    enc_lengths,
):
    rows_here = tokens.shape[0]
    step_value = jnp.float32(STEP)
    branch_scale = step_value / (step_value + ramp_steps)
    self_mask = mask_maker(bucket_shift[0], seq_lengths[0], rows_here, True)
    cross_mask = mask_maker(bucket_shift[0], enc_lengths[0], rows_here, False)
    self_whole, self_proj = (
        lax.all_gather(self_qkv, "fsdp", axis=1, tiled=True),
        lax.all_gather(self_out, "fsdp", axis=0, tiled=True),
    )
    projected = jnp.einsum(
        "td,kde->kte", tokens, self_whole, preferred_element_type=jnp.float32
    ).astype(jnp.bfloat16)
    queries, key_rows, value_rows = (projected[0], projected[1], projected[2])
    mixed, self_totals = attend_forward(queries, key_rows, value_rows, self_mask)
    mixed = mixed.astype(jnp.bfloat16)
    normal_one, inverse_one = layer_stats(
        tokens.astype(jnp.float32) + jnp.dot(mixed, self_proj, preferred_element_type=jnp.float32)
    )
    first = normal_one * norm_gain[0] + norm_bias[0]
    first_low = first.astype(jnp.bfloat16)
    cross_whole, cross_proj = (
        lax.all_gather(cross_qkv, "fsdp", axis=1, tiled=True),
        lax.all_gather(cross_out, "fsdp", axis=0, tiled=True),
    )
    cross_queries = jnp.dot(first_low, cross_whole[0], preferred_element_type=jnp.float32).astype(
        jnp.bfloat16
    )
    cross_pairs = jnp.einsum(
        "td,kde->kte", encoder, cross_whole[1:], preferred_element_type=jnp.float32
    ).astype(jnp.bfloat16)
    joined, cross_totals = attend_forward(cross_queries, cross_pairs[0], cross_pairs[1], cross_mask)
    joined = joined.astype(jnp.bfloat16)
    normal_two, inverse_two = layer_stats(
        first + jnp.dot(joined, cross_proj, preferred_element_type=jnp.float32)
    )
    second = normal_two * norm_gain[1] + norm_bias[1]
    second_low = second.astype(jnp.bfloat16)
    ffn_whole_in, ffn_whole_out = (
        lax.all_gather(ffn_in, "fsdp", axis=0, tiled=True),
        lax.all_gather(ffn_out, "fsdp", axis=0, tiled=True),
    )
    inner = jnp.dot(second_low, ffn_whole_in, preferred_element_type=jnp.float32)
    active = gelu_exact(inner).astype(jnp.bfloat16)
    narrow = jnp.dot(second_low, adapt_down, preferred_element_type=jnp.float32) + down_bias
    narrow_act = jax.nn.silu(narrow).astype(jnp.bfloat16)
    branch = jnp.dot(narrow_act, adapt_up, preferred_element_type=jnp.float32) + up_bias
    sum_three = (
        second
        + jnp.dot(active, ffn_whole_out, preferred_element_type=jnp.float32)
        + branch_scale * branch
    )
    normal_three, inverse_three = layer_stats(sum_three)
    output = (normal_three * norm_gain[2] + norm_bias[2]).astype(jnp.bfloat16)
    grad_three, gain_three, bias_three = norm_back(
        cotangent.astype(jnp.float32), normal_three, inverse_three, norm_gain[2]
    )
    grad_feed = grad_three.astype(jnp.bfloat16)
    grad_branch = (branch_scale * grad_three).astype(jnp.bfloat16)
    grad_up = jnp.einsum("ta,td->ad", narrow_act, grad_branch, preferred_element_type=jnp.float32)
    grad_upb = jnp.sum(grad_branch.astype(jnp.float32), 0)
    grad_act = jnp.einsum("td,ad->ta", grad_branch, adapt_up, preferred_element_type=jnp.float32)
    grad_narrow = jax.vjp(jax.nn.silu, narrow)[1](grad_act)[0].astype(jnp.bfloat16)
    grad_down = jnp.einsum("td,ta->da", second_low, grad_narrow, preferred_element_type=jnp.float32)
    grad_downb = jnp.sum(grad_narrow.astype(jnp.float32), 0)
    ffn_back_in, ffn_back_out = (ffn_whole_in, ffn_whole_out)
    grad_active = jnp.einsum(
        "td,fd->tf", grad_feed, ffn_back_out, preferred_element_type=jnp.float32
    )
    grad_inner = jax.vjp(gelu_exact, inner)[1](grad_active)[0].astype(jnp.bfloat16)
    grad_second = (
        grad_three
        + jnp.einsum("tf,df->td", grad_inner, ffn_back_in, preferred_element_type=jnp.float32)
        + jnp.einsum("ta,da->td", grad_narrow, adapt_down, preferred_element_type=jnp.float32)
    )
    grad_two, gain_two, bias_two = norm_back(grad_second, normal_two, inverse_two, norm_gain[1])
    cross_back, cross_back_proj = (cross_whole, cross_proj)
    grad_joined = jnp.einsum(
        "td,ed->te",
        grad_two.astype(jnp.bfloat16),
        cross_back_proj,
        preferred_element_type=jnp.float32,
    ).astype(jnp.bfloat16)
    grad_cquery, grad_ckeys, grad_cvalues = attend_backward(
        cross_queries, cross_pairs[0], cross_pairs[1], grad_joined, cross_totals, cross_mask
    )
    grad_first = grad_two + jnp.einsum(
        "te,de->td", grad_cquery, cross_back[0], preferred_element_type=jnp.float32
    )
    grad_encoder = (
        jnp.einsum("te,de->td", grad_ckeys, cross_back[1], preferred_element_type=jnp.float32)
        + jnp.einsum("te,de->td", grad_cvalues, cross_back[2], preferred_element_type=jnp.float32)
    ).astype(jnp.bfloat16)
    grad_one, gain_one, bias_one = norm_back(grad_first, normal_one, inverse_one, norm_gain[0])
    self_back, self_back_proj = (self_whole, self_proj)
    grad_mixed = jnp.einsum(
        "td,ed->te",
        grad_one.astype(jnp.bfloat16),
        self_back_proj,
        preferred_element_type=jnp.float32,
    ).astype(jnp.bfloat16)
    grad_query, grad_keys, grad_values = attend_backward(
        queries, key_rows, value_rows, grad_mixed, self_totals, self_mask
    )
    grad_tokens = grad_one + jnp.einsum(
        "te,de->td", grad_query, self_back[0], preferred_element_type=jnp.float32
    )
    grad_tokens = grad_tokens + jnp.einsum(
        "te,de->td", grad_keys, self_back[1], preferred_element_type=jnp.float32
    )
    grad_tokens = (
        grad_tokens
        + jnp.einsum("te,de->td", grad_values, self_back[2], preferred_element_type=jnp.float32)
    ).astype(jnp.bfloat16)
    gain_grads = jnp.stack([gain_one, gain_two, gain_three])
    bias_grads = jnp.stack([bias_one, bias_two, bias_three])
    summed = lax.psum(
        (grad_down, grad_downb, grad_up, grad_upb, gain_grads, bias_grads), ("fsdp", "dp")
    )
    return (
        output,
        grad_tokens,
        grad_encoder,
        summed[0],
        summed[1],
        summed[2],
        summed[3],
        summed[4],
        summed[5],
    )


def solution(mesh):
    placed = (
        P(("fsdp", "dp"), None),
        P(("fsdp", "dp"), None),
        P(("fsdp", "dp"), None),
        P(None, "fsdp", None),
        P("fsdp", None),
        P(None, "fsdp", None),
        P("fsdp", None),
        P("fsdp", None),
        P("fsdp", None),
        P(),
        P(),
        P(),
        P(),
        P(),
        P(),
        P(("fsdp", "dp")),
        P(("fsdp", "dp"), None),
        P(("fsdp", "dp"), None),
    )
    return jax.shard_map(
        local,
        mesh=mesh,
        in_specs=placed,
        out_specs=(
            P(("fsdp", "dp"), None),
            P(("fsdp", "dp"), None),
            P(("fsdp", "dp"), None),
            P(),
            P(),
            P(),
            P(),
            P(),
            P(),
        ),
        check_vma=False,
    )
```

profile of v0, /device:TPU:0, one launch (start us, length us, event | category | flops | bytes accessed | tf_op | source)
XLA Modules:
  0.0 671.9 jit_solution(5962567609360192254)
XLA Ops:
  14.3 60.7 %all-gather.7.cloned.1.call-done = bf16[3,1024,1024]{2,1,0:T(8,128)(2,1)} async-done(((bf16[3,64,1024]{2,1,0:T(8,128)(2,1)}), bf16[3,1024,1024]{2,1,0:T(8,128)(2,1)}) %all-gather.7.cloned.1.call-update) | async-done | bytes 6291472 | tf_op jit(solution)/shard_map/all_gather | solution.py:167
  74.9 6.6 convert_bitcast_fusion
  81.8 7.5 %fusion.77 = (f32[16,512]{1,0:T(8,128)S(1)}, f32[16,512,512]{1,2,0:T(8,128)}) fusion(bf16[512,16,64]{0,2,1:T(8,128)(2,1)S(1)} %bitcast.153, bf16[512,16,64]{0,2,1:T(8,128)(2,1)S(1)} %bitcast.143, pred[512,512]{0,1:T(8,128)(4,1)S(1)} %get-tuple-element.169), kind=kOutput, calls=%fused_computation.163 | convolution fusion | flops 549445632 | bytes 19169280 | tf_op jit(solution)/shard_map/while/body/eval_jaxpr/thd,shd->hts/dot_general | solution.py:70
  89.2 8.3 %fusion = f32[16,512]{1,0:T(8,128)S(1)} fusion(f32[16,512,512]{1,2,0:T(8,128)} %get-tuple-element.184, f32[16,512]{1,0:T(8,128)S(1)} %get-tuple-element.170), kind=kLoop, calls=%fused_computation.12 | loop fusion | flops 8380416 | bytes 16842752 | tf_op jit(solution)/shard_map/while/body/eval_jaxpr/reduce_sum | solution.py:76
  97.6 8.7 %fusion.40 = bf16[16,64,512]{2,1,0:T(8,128)(2,1)} fusion(bf16[512,16,64]{0,2,1:T(8,128)(2,1)S(1)} %bitcast.155, f32[16,512,512]{1,2,0:T(8,128)} %get-tuple-element.184, f32[16,512]{1,0:T(8,128)S(1)} %fusion, f32[16,512]{1,0:T(8,128)S(1)} %get-tuple-element.170), kind=kOutput, calls=%fused_computation.101 | convolution fusion | flops 549978112 | bytes 18939904 | tf_op jit(solution)/shard_map/while/body/eval_jaxpr/hts,shd->thd/dot_general | solution.py:78
  106.3 10.9 %all-gather.9.cloned.1.call-done = bf16[1024,1024]{1,0:T(8,128)(2,1)} async-done(((bf16[64,1024]{1,0:T(8,128)(2,1)}), bf16[1024,1024]{1,0:T(8,128)(2,1)}) %all-gather.9.cloned.1.call-update) | async-done | bytes 2097168 | tf_op jit(solution)/shard_map/all_gather | solution.py:168
  121.0 59.0 %all-gather.11.cloned.1.call-done = bf16[3,1024,1024]{2,1,0:T(8,128)(2,1)} async-done(((bf16[3,64,1024]{2,1,0:T(8,128)(2,1)}), bf16[3,1024,1024]{2,1,0:T(8,128)(2,1)}) %all-gather.11.cloned.1.call-update) | async-done | bytes 6291472 | tf_op jit(solution)/shard_map/all_gather | solution.py:182
  180.1 3.9 fusion.41
  185.6 5.0 convert_bitcast_fusion.1
  190.8 7.5 %fusion.79 = (f32[16,512]{1,0:T(8,128)S(1)}, f32[16,512,512]{1,2,0:T(8,128)}) fusion(bf16[512,16,64]{0,2,1:T(8,128)(2,1)S(1)} %bitcast.147, bf16[512,16,64]{0,2,1:T(8,128)(2,1)S(1)} %bitcast.145, pred[512,512]{0,1:T(8,128)(4,1)S(1)} %get-tuple-element.168), kind=kOutput, calls=%fused_computation.165 | convolution fusion | flops 549445632 | bytes 19169280 | tf_op jit(solution)/shard_map/while/body/eval_jaxpr/thd,shd->hts/dot_general | solution.py:70
  198.3 8.3 %fusion.1 = f32[16,512]{1,0:T(8,128)S(1)} fusion(f32[16,512,512]{1,2,0:T(8,128)} %get-tuple-element.188, f32[16,512]{1,0:T(8,128)S(1)} %get-tuple-element.187), kind=kLoop, calls=%fused_computation.13 | loop fusion | flops 8380416 | bytes 16842752 | tf_op jit(solution)/shard_map/while/body/eval_jaxpr/reduce_sum | solution.py:76
  206.5 7.6 %fusion.39 = bf16[16,64,512]{2,1,0:T(8,128)(2,1)S(1)} fusion(bf16[512,16,64]{0,2,1:T(8,128)(2,1)S(1)} %bitcast.157, f32[16,512,512]{1,2,0:T(8,128)} %get-tuple-element.188, f32[16,512]{1,0:T(8,128)S(1)} %fusion.1, f32[16,512]{1,0:T(8,128)S(1)} %get-tuple-element.187), kind=kOutput, calls=%fused_computation.100 | convolution fusion | flops 549978112 | bytes 18939904 | tf_op jit(solution)/shard_map/while/body/eval_jaxpr/hts,shd->thd/dot_general | solution.py:78
  214.1 8.0 %all-gather.13.cloned.1.call-done = bf16[1024,1024]{1,0:T(8,128)(2,1)} async-done(((bf16[64,1024]{1,0:T(8,128)(2,1)}), bf16[1024,1024]{1,0:T(8,128)(2,1)}) %all-gather.13.cloned.1.call-update) | async-done | bytes 2097168 | tf_op jit(solution)/shard_map/all_gather | solution.py:183
  229.5 68.3 %all-gather.15.cloned.1.call-done = bf16[1024,4096]{1,0:T(8,128)(2,1)} async-done(((bf16[64,4096]{1,0:T(8,128)(2,1)}), bf16[1024,4096]{1,0:T(8,128)(2,1)}) %all-gather.15.cloned.1.call-update) | async-done | bytes 8388624 | tf_op jit(solution)/shard_map/all_gather | solution.py:199
  297.8 25.0 %fusion.4 = (f32[512,4096]{1,0:T(8,128)}, f32[512,4096]{1,0:T(8,128)}) fusion(bf16[512,1024]{1,0:T(8,128)(2,1)S(1)} %fusion.35, bf16[1024,4096]{1,0:T(8,128)(2,1)} %all-gather.15.cloned.1.call-done), kind=kOutput, calls=%fused_computation.17 | convolution fusion | flops 4424990720 | bytes 26214400 | tf_op jit(solution)/shard_map/dot_general | solution.py:202
  322.8 50.2 %all-gather.17.cloned.1.call-done = bf16[4096,1024]{1,0:T(8,128)(2,1)} async-done(((bf16[256,1024]{1,0:T(8,128)(2,1)}), bf16[4096,1024]{1,0:T(8,128)(2,1)}) %all-gather.17.cloned.1.call-update) | async-done | bytes 8388624 | tf_op jit(solution)/shard_map/all_gather | solution.py:200
  373.0 11.0 %fusion.18 = f32[512,1024]{1,0:T(8,128)S(1)} fusion(bf16[4096,1024]{1,0:T(8,128)(2,1)} %all-gather.17.cloned.1.call-done, f32[512,4096]{1,0:T(8,128)} %get-tuple-element.191, f32[512,4096]{1,0:T(8,128)} %get-tuple-element.192), kind=kOutput, calls=%fused_computation.39 | convolution fusion | flops 4301258752 | bytes 27262976 | tf_op jit(solution)/shard_map/dot_general | solution.py:209
  396.4 19.1 %fusion.20 = f32[512,1024]{1,0:T(8,128)} fusion(bf16[1024,4096]{1,0:T(8,128)(2,1)} %all-gather.15.cloned.1.call-done, f32[512,4096]{1,0:T(8,128)} %get-tuple-element.191, f32[512,4096]{1,0:T(8,128)} %get-tuple-element.192, bf16[4096,1024]{1,0:T(8,128)(2,1)} %all-gather.17.cloned.1.call-done, f32[512,1024]{1,0:T(8,128)} %copy-done.15), kind=kOutput, calls=%fused_computation.41 | convolution fusion | flops 8619819008 | bytes 37748736 | tf_op jit(solution)/shard_map/tf,df->td/dot_general | solution.py:232
  415.5 4.6 multiply_reduce_fusion.2
  425.5 9.6 %fusion.42 = bf16[16,64,512]{2,1,0:T(8,128)(2,1)} fusion(bf16[512,16,64]{0,2,1:T(8,128)(2,1)S(1)} %bitcast.149, f32[16,512,512]{1,2,0:T(8,128)} %get-tuple-element.188, f32[16,512]{1,0:T(8,128)S(1)} %log_add_fusion.1), kind=kOutput, calls=%fused_computation.105 | convolution fusion | flops 545783808 | bytes 18907136 | tf_op jit(solution)/shard_map/while/body/eval_jaxpr/hts,thd->shd/dot_general | solution.py:121
  435.1 13.9 %multiply_reduce_fusion.1 = (f32[16,512]{1,0:T(8,128)}, f32[16,512,512]{1,2,0:T(8,128)}) fusion(f32[16,512,512]{1,2,0:T(8,128)} %get-tuple-element.188, f32[16,512]{1,0:T(8,128)} %copy-done.31, bf16[512,16,64]{0,2,1:T(8,128)(2,1)S(1)} %bitcast.150, bf16[512,16,64]{0,2,1:T(8,128)(2,1)} %bitcast.158), kind=kOutput, calls=%fused_computation.4 | convolution fusion | flops 549445632 | bytes 35717120 | tf_op jit(solution)/shard_map/while/body/eval_jaxpr/thd,shd->hts/dot_general | solution.py:105
  449.0 10.7 %multiply_convert_fusion.1 = bf16[16,512,512]{1,2,0:T(8,128)(2,1)} fusion(f32[16,512,512]{1,2,0:T(8,128)} %get-tuple-element.197, f32[16,512,512]{1,2,0:T(8,128)S(1)} %bitcast.140, f32[16,512]{1,0:T(8,128)} %get-tuple-element.196, f32[16,512]{1,0:T(8,128)} %copy-done.31), kind=kLoop, calls=%fused_computation.3 | loop fusion | flops 16777216 | bytes 42008576 | tf_op jit(solution)/shard_map/while/body/eval_jaxpr/convert_element_type | solution.py:109
  459.8 7.5 %multiply_convert_fusion.4 = bf16[16,64,512]{2,1,0:T(8,128)(2,1)} fusion(bf16[512,16,64]{0,2,1:T(8,128)(2,1)} %bitcast.148, bf16[16,512,512]{1,2,0:T(8,128)(2,1)} %multiply_convert_fusion.1), kind=kOutput, calls=%fused_computation.68 | convolution fusion | flops 537919488 | bytes 10485760 | tf_op jit(solution)/shard_map/while/body/eval_jaxpr/hts,thd->shd/dot_general | solution.py:116
  470.1 5.0 multiply_reduce_fusion.3
  478.6 9.6 %fusion.45 = bf16[16,64,512]{2,1,0:T(8,128)(2,1)} fusion(bf16[512,16,64]{0,2,1:T(8,128)(2,1)S(1)} %bitcast.151, f32[16,512,512]{1,2,0:T(8,128)} %get-tuple-element.184, f32[16,512]{1,0:T(8,128)S(1)} %copy-done.30), kind=kOutput, calls=%fused_computation.106 | convolution fusion | flops 545783808 | bytes 18907136 | tf_op jit(solution)/shard_map/while/body/eval_jaxpr/hts,thd->shd/dot_general | solution.py:121
  488.2 13.9 %multiply_reduce_fusion = (f32[16,512]{1,0:T(8,128)}, f32[16,512,512]{1,2,0:T(8,128)}) fusion(f32[16,512,512]{1,2,0:T(8,128)} %get-tuple-element.184, f32[16,512]{1,0:T(8,128)} %log_add_fusion, bf16[512,16,64]{0,2,1:T(8,128)(2,1)S(1)} %bitcast.152, bf16[512,16,64]{0,2,1:T(8,128)(2,1)} %bitcast.156), kind=kOutput, calls=%fused_computation.1 | convolution fusion | flops 549445632 | bytes 35717120 | tf_op jit(solution)/shard_map/while/body/eval_jaxpr/thd,shd->hts/dot_general | solution.py:105
  502.2 10.8 %multiply_convert_fusion = bf16[16,512,512]{1,2,0:T(8,128)(2,1)} fusion(f32[16,512,512]{1,2,0:T(8,128)} %get-tuple-element.200, f32[16,512,512]{1,2,0:T(8,128)S(1)} %bitcast.138, f32[16,512]{1,0:T(8,128)} %get-tuple-element.199, f32[16,512]{1,0:T(8,128)} %log_add_fusion), kind=kLoop, calls=%fused_computation | loop fusion | flops 16777216 | bytes 42008576 | tf_op jit(solution)/shard_map/while/body/eval_jaxpr/convert_element_type | solution.py:109
  513.0 6.0 multiply_convert_fusion.5
  519.8 40.1 %all-reduce = (f32[512]{0:T(512)}, f32[1024]{0:T(1024)}, f32[3,1024]{1,0:T(4,128)}, f32[3,1024]{1,0:T(4,128)}) all-reduce(f32[512]{0:T(512)S(1)} %copy-done.49, f32[1024]{0:T(1024)S(1)} %copy-done.37, f32[3,1024]{1,0:T(4,128)S(1)} %pad_maximum_fusion, ...), channel_id=1, replica_groups=mesh['fsdp'=16,'dp'=2] {'fsdp','dp'}, use_global_device_ids=true, to_apply=%region_22.23 | all-reduce | flops 7680 | bytes 61440 | tf_op jit(solution)/shard_map/psum | solution.py:276
  569.1 4.0 add_convert_fusion.2
  575.4 4.7 add_convert_fusion.3
  580.0 80.2 %all-reduce.4.cloned.1.call-done = (f32[1024,512]{1,0:T(8,128)}, f32[512,1024]{1,0:T(8,128)}) async-done(((f32[1024,512]{1,0:T(8,128)}, f32[512,1024]{1,0:T(8,128)}), (f32[1024,512]{1,0:T(8,128)}, f32[512,1024]{1,0:T(8,128)})) %all-reduce.4.cloned.1.call-update) | async-done | bytes 4194320 | tf_op jit(solution)/shard_map/psum | solution.py:276
  (219 shorter events, 60.2 us)
Async XLA Ops:
  7.2 178.4 %copy-start = (bf16[512,1024]{1,0:T(8,128)(2,1)S(1)}, bf16[512,1024]{1,0:T(8,128)(2,1)}, u32[]{:S(2)}) copy-start(bf16[512,1024]{1,0:T(8,128)(2,1)} %param.19) | copy-start | bytes 3145732
  7.2 67.7 %copy-start.29 = (bf16[512,1024]{1,0:T(8,128)(2,1)S(1)}, bf16[512,1024]{1,0:T(8,128)(2,1)}, u32[]{:S(2)}) copy-start(bf16[512,1024]{1,0:T(8,128)(2,1)} %param.18) | copy-start | bytes 3145732
  7.2 67.7 %all-gather.7.cloned.1.call-start = ((), (), s32[]{:S(2)}) async-start(), calls=%async_computation | async-start | bytes 6684672 | tf_op jit(solution)/shard_map/all_gather | solution.py:167
  8.0 109.1 %all-gather.9.cloned.1.call-start = ((), (), s32[]{:S(2)}) async-start(), calls=%async_computation.1 | async-start | bytes 2228224 | tf_op jit(solution)/shard_map/all_gather | solution.py:168
  8.7 171.3 %all-gather.11.cloned.1.call-start = ((), (), s32[]{:S(2)}) async-start(), calls=%async_computation.2 | async-start | bytes 6684672 | tf_op jit(solution)/shard_map/all_gather | solution.py:182
  9.5 212.6 %all-gather.13.cloned.1.call-start = ((), (), s32[]{:S(2)}) async-start(), calls=%async_computation.3 | async-start | bytes 2228224 | tf_op jit(solution)/shard_map/all_gather | solution.py:183
  10.0 287.8 %all-gather.15.cloned.1.call-start = ((), (), s32[]{:S(2)}) async-start(), calls=%async_computation.4 | async-start | bytes 8912896 | tf_op jit(solution)/shard_map/all_gather | solution.py:199
  10.6 362.4 %all-gather.17.cloned.1.call-start = ((), (), s32[]{:S(2)}) async-start(), calls=%async_computation.5 | async-start | bytes 8912896 | tf_op jit(solution)/shard_map/all_gather | solution.py:200
  11.2 649.0 %all-reduce.4.cloned.1.call-start = ((), (), s32[]{:S(2)}) async-start(), calls=%async_computation.6 | async-start | bytes 8388608 | tf_op jit(solution)/shard_map/psum | solution.py:276
  13.0 209.1 %copy-start.46 = (f32[1,1024]{1,0:T(1,128)}, f32[1,1024]{1,0:T(1,128)S(1)}, u32[]{:S(2)}) copy-start(f32[1,1024]{1,0:T(1,128)S(1)} %get-tuple-element.163) | copy-start | bytes 12292
  81.8 15.8 %copy-start.16 = (bf16[1,512,1024]{1,2,0:T(8,128)(2,1)}, bf16[1,512,1024]{1,2,0:T(8,128)(2,1)S(1)}, u32[]{:S(2)}) copy-start(bf16[1,512,1024]{1,2,0:T(8,128)(2,1)S(1)} %get-tuple-element.158) | copy-start | bytes 3145732
  120.6 59.4 %copy-start.12 = (f32[512,1024]{1,0:T(8,128)}, f32[512,1024]{1,0:T(8,128)S(1)}, u32[]{:S(2)}) copy-start(f32[512,1024]{1,0:T(8,128)S(1)} %get-tuple-element.186) | copy-start | bytes 6291460
  120.7 101.4 %copy-start.41 = (f32[512]{0:T(512)}, f32[512]{0:T(512)S(1)}, u32[]{:S(2)}) copy-start(f32[512]{0:T(512)S(1)} %broadcast_multiply_fusion.8) | copy-start | bytes 6148
  121.0 101.1 %copy-start.50 = (f32[512]{0:T(512)}, f32[512]{0:T(512)S(1)}, u32[]{:S(2)}) copy-start(f32[512]{0:T(512)S(1)} %add_rsqrt_fusion.2) | copy-start | bytes 6148
  190.8 15.7 %copy-start.17 = (bf16[1,512,1024]{1,2,0:T(8,128)(2,1)}, bf16[1,512,1024]{1,2,0:T(8,128)(2,1)S(1)}, u32[]{:S(2)}) copy-start(bf16[1,512,1024]{1,2,0:T(8,128)(2,1)S(1)} %get-tuple-element.161) | copy-start | bytes 3145732
  225.8 194.4 %copy-start.3 = (f32[512,1024]{1,0:T(8,128)}, f32[512,1024]{1,0:T(8,128)S(1)}, u32[]{:S(2)}) copy-start(f32[512,1024]{1,0:T(8,128)S(1)} %get-tuple-element.190) | copy-start | bytes 6291460
  226.8 198.7 %copy-start.31 = (f32[16,512]{1,0:T(8,128)}, f32[16,512]{1,0:T(8,128)S(1)}, u32[]{:S(2)}) copy-start(f32[16,512]{1,0:T(8,128)S(1)} %log_add_fusion.1) | copy-start | bytes 98308
  373.0 11.0 %copy-start.60 = (bf16[512,1024]{1,0:T(8,128)(2,1)S(1)}, bf16[512,1024]{1,0:T(8,128)(2,1)}, u32[]{:S(2)}) copy-start(bf16[512,1024]{1,0:T(8,128)(2,1)} %param.29) | copy-start | bytes 3145732
  373.0 11.0 %copy-start.61 = (f32[1024]{0:T(1024)S(1)}, f32[1024]{0:T(1024)}, u32[]{:S(2)}) copy-start(f32[1024]{0:T(1024)} %param.30) | copy-start | bytes 12292
  373.0 11.0 %copy-start.65 = (f32[512,512]{1,0:T(8,128)S(1)}, f32[512,512]{1,0:T(8,128)}, u32[]{:S(2)}) copy-start(f32[512,512]{1,0:T(8,128)} %convolution_add_fusion) | copy-start | bytes 3145732
  396.4 19.1 %copy-start.20 = (bf16[512,512]{1,0:T(8,128)(2,1)S(1)}, bf16[512,512]{1,0:T(8,128)(2,1)}, u32[]{:S(2)}) copy-start(bf16[512,512]{1,0:T(8,128)(2,1)} %copy-done.19) | copy-start | bytes 1572868
  425.5 23.5 %slice-start.4 = ((s8[16777216]{0:T(1024)(128)(4,1)}), s8[4194304]{0:T(1024)(128)(4,1)S(1)}, s32[]{:S(2)}) async-start(s8[16777216]{0:T(1024)(128)(4,1)} %bitcast.139), calls=%async_computation.11 | async-start | bytes 8388608
  425.5 23.5 %slice-start.5 = ((s8[16777216]{0:T(1024)(128)(4,1)}), s8[4194304]{0:T(1024)(128)(4,1)S(1)}, s32[]{:S(2)}) async-start(s8[16777216]{0:T(1024)(128)(4,1)} %bitcast.139), calls=%async_computation.12 | async-start | bytes 8388608
  435.1 13.9 %slice-start.6 = ((s8[16777216]{0:T(1024)(128)(4,1)}), s8[4194304]{0:T(1024)(128)(4,1)S(1)}, s32[]{:S(2)}) async-start(s8[16777216]{0:T(1024)(128)(4,1)} %bitcast.139), calls=%async_computation.13 | async-start | bytes 8388608
  435.1 13.9 %slice-start.7 = ((s8[16777216]{0:T(1024)(128)(4,1)}), s8[4194304]{0:T(1024)(128)(4,1)S(1)}, s32[]{:S(2)}) async-start(s8[16777216]{0:T(1024)(128)(4,1)} %bitcast.139), calls=%async_computation.14 | async-start | bytes 8388608
  478.6 23.5 %slice-start = ((s8[16777216]{0:T(1024)(128)(4,1)}), s8[4194304]{0:T(1024)(128)(4,1)S(1)}, s32[]{:S(2)}) async-start(s8[16777216]{0:T(1024)(128)(4,1)} %bitcast.137), calls=%async_computation.7 | async-start | bytes 8388608
  478.6 23.5 %slice-start.1 = ((s8[16777216]{0:T(1024)(128)(4,1)}), s8[4194304]{0:T(1024)(128)(4,1)S(1)}, s32[]{:S(2)}) async-start(s8[16777216]{0:T(1024)(128)(4,1)} %bitcast.137), calls=%async_computation.8 | async-start | bytes 8388608
  488.2 13.9 %slice-start.2 = ((s8[16777216]{0:T(1024)(128)(4,1)}), s8[4194304]{0:T(1024)(128)(4,1)S(1)}, s32[]{:S(2)}) async-start(s8[16777216]{0:T(1024)(128)(4,1)} %bitcast.137), calls=%async_computation.9 | async-start | bytes 8388608
  488.2 13.9 %slice-start.3 = ((s8[16777216]{0:T(1024)(128)(4,1)}), s8[4194304]{0:T(1024)(128)(4,1)S(1)}, s32[]{:S(2)}) async-start(s8[16777216]{0:T(1024)(128)(4,1)} %bitcast.137), calls=%async_computation.10 | async-start | bytes 8388608
  502.1 10.8 %copy-start.11 = (bf16[1,512,1024]{1,2,0:T(8,128)(2,1)S(1)}, bf16[1,512,1024]{1,2,0:T(8,128)(2,1)}, u32[]{:S(2)}) copy-start(bf16[1,512,1024]{1,2,0:T(8,128)(2,1)} %copy-done.10) | copy-start | bytes 3145732
  519.1 40.9 %copy-start.26 = (bf16[16,64,512]{2,1,0:T(8,128)(2,1)S(1)}, bf16[16,64,512]{2,1,0:T(8,128)(2,1)}, u32[]{:S(2)}) copy-start(bf16[16,64,512]{2,1,0:T(8,128)(2,1)} %fusion.42) | copy-start | bytes 3145732
  562.9 10.2 %slice-start.8 = ((s8[8388608]{0:T(1024)(128)(4,1)}), s8[4194304]{0:T(1024)(128)(4,1)S(1)}, s32[]{:S(2)}) async-start(s8[8388608]{0:T(1024)(128)(4,1)} %bitcast.141), calls=%async_computation.15 | async-start | bytes 8388608
  (51 other events, 158.5 us)
Sparse Core Ops, SparseCore 0:
  10.3 64.6 all-gather.6
  77.1 39.9 all-gather.8
  119.3 60.6 all-gather.10
  182.1 39.9 all-gather.12
  224.1 73.6 all-gather.14
  299.8 73.1 all-gather.16
  519.2 140.9 all-reduce.3
where the time goes:
time: 681 us; the launch traced here: 672 us
  waiting for transfers between devices  341 us (50%)
  matrix products  212 us (31%)
  other arithmetic  45.4 us (7%)
  blocking collectives  40.1 us (6%)
  local copies, waits for them, and re-layouts  16.9 us (2%)
  between operations  15.9 us (2%)
    psum x1, waiting for transfers between devices, local(): lax.psum((grad_down, grad_downb, grad_up, grad_upb, gain_grads, bias_grad...  80.2 us
    all_gather x1, waiting for transfers between devices, local(): lax.all_gather(ffn_in, 'fsdp', axis=0, tiled=True)  68.3 us
    all_gather x1, waiting for transfers between devices, local(): lax.all_gather(self_qkv, 'fsdp', axis=1, tiled=True)  60.7 us
    all_gather x1, waiting for transfers between devices, local(): lax.all_gather(cross_qkv, 'fsdp', axis=1, tiled=True)  59 us
    all_gather x1, waiting for transfers between devices, local(): lax.all_gather(ffn_out, 'fsdp', axis=0, tiled=True)  50.2 us
    psum x1, blocking collectives, local(): lax.psum((grad_down, grad_downb, grad_up, grad_upb, gain_grads, bias_grad...  40.1 us
    dot_general x2, matrix products, one_block(): jnp.einsum('thd,shd->hts', grad_heads, value_heads, preferred_element_typ...  27.8 us
    dot_general x1, matrix products, local(): jnp.dot(second_low, ffn_whole_in, preferred_element_type=jnp.float32)  25 us
  transfers between devices with their start and end apart: 7, of which 7 were waited for; matrix products, arithmetic and copies ran while one was open for 18% of the time, Pallas kernels for 0%

commit v1 on v0

--- a/solution.py
+++ b/solution.py
@@ -1,6 +1,10 @@
+import functools
+
 import jax
 import jax.numpy as jnp
 from jax import lax
+from jax.experimental import pallas as pl
+from jax.experimental.pallas import tpu as pltpu
 from jax.sharding import PartitionSpec as P
 
 HEADS = 16
@@ -136,6 +140,266 @@
         grad_keys.reshape(key_rows.shape[0], -1).astype(jnp.bfloat16),
         grad_values.reshape(value_rows.shape[0], -1).astype(jnp.bfloat16),
     )
+
+
+MESH = pl.DeviceIdType.MESH
+LINE = 4
+
+
+def nearest(place, count, rank):
+    under, over = place, count - 1 - place
+    both = jnp.minimum(under, over)
+    paired = jnp.where(rank % 2 == 1, place - (rank + 1) // 2, place + rank // 2)
+    alone = jnp.where(over > under, place + rank - both, place - (rank - both))
+    return jnp.where(rank <= 2 * both, paired, alone)
+
+
+class Gather:
+    def __init__(self, count, views, send_sem, recv_sem):
+        self.views, self.send_sem, self.recv_sem = views, send_sem, recv_sem
+        self.line = min(LINE, count // 2)
+        self.wide = count // (2 * self.line)
+        index = lax.axis_index("fsdp")
+        self.dp = lax.axis_index("dp")
+        self.core = index % 2
+        self.x = (index // 2) % self.wide
+        self.z = index // (2 * self.wide)
+        self.plane = self.dp % 2
+        self.other_core = (self.place(self.z, self.x, 1 - self.core), self.dp)
+        self.other_plane = (index, self.dp + 1 - 2 * self.plane)
+        self.sends = []
+        self.counts = [0] * len(views)
+
+    def place(self, z, x, core):
+        return (z * self.wide + x) * 2 + core
+
+    def enter(self):
+        barrier = pltpu.get_barrier_semaphore()
+
+        def greet(target):
+            pl.semaphore_signal(barrier, inc=1, device_id=target, device_id_type=MESH)
+
+        greet(self.other_core)
+        greet(self.other_plane)
+        total = 2
+        for along, size, target in (
+            (self.z, self.line, lambda to: (self.place(to, self.x, self.core), self.dp)),
+            (self.x, self.wide, lambda to: (self.place(self.z, to, self.core), self.dp)),
+        ):
+            for step in (-1, 1):
+                inside = (along + step >= 0) & (along + step < size)
+
+                @pl.when(inside)
+                def _():
+                    greet(target(along + step))
+
+                total = total + inside.astype(jnp.int32)
+        pl.semaphore_wait(barrier, total)
+
+    def send(self, phase, core, z, x, kind, first, units, target, when=None):
+        view = self.views[phase](self.place(z, x, core), first, units)
+        slot = self.counts[phase]
+        self.counts[phase] += 1
+        copy = pltpu.make_async_remote_copy(
+            src_ref=view,
+            dst_ref=view,
+            send_sem=self.send_sem.at[phase, slot],
+            recv_sem=self.recv_sem.at[phase, core, z * self.wide + x, kind],
+            device_id=target,
+            device_id_type=MESH,
+        )
+        if when is None:
+            copy.start()
+        else:
+            pl.when(when)(copy.start)
+        self.sends.append((copy, when))
+
+    def arrive(self, phase, core, z, x, kind, first, units):
+        view = self.views[phase](self.place(z, x, core), first, units)
+        pltpu.make_async_copy(view, view, self.recv_sem.at[phase, core, z * self.wide + x, kind]).wait()
+
+    def spans(self, other):
+        p = self.plane
+        if other:
+            return ((2 * p, 2), (4 + p, 3), (2 - 2 * p, 2), (7 - 3 * p, 1))
+        return ((2 * p, 2), (4, 4), (2 - 2 * p, 2))
+
+    def along_z(self, step):
+        return (self.place(self.z + step, self.x, self.core), self.dp)
+
+    def along_x(self, step):
+        return (self.place(self.z, self.x + step, self.core), self.dp)
+
+    def own(self, phase):
+        at = (phase, self.core, self.z, self.x)
+        spans = self.spans(False)
+        cross = self.spans(True)
+        for kind in (0, 1):
+            self.send(*at, kind, *spans[kind], self.along_z(1), self.z < self.line - 1)
+            self.send(*at, kind, *spans[kind], self.along_z(-1), self.z > 0)
+            self.over_x(at, kind, cross[kind])
+        self.send(*at, 0, 0, 8, self.other_core)
+
+    def over_x(self, at, kind, span):
+        if self.wide == 2:
+            self.send(*at, kind, *span, self.along_x(1 - 2 * self.x))
+            return
+        self.send(*at, kind, *span, self.along_x(1), self.x < self.wide - 1)
+        self.send(*at, kind, *span, self.along_x(-1), self.x > 0)
+
+    def ticks(self, phase):
+        for step in range(1, self.line + self.wide):
+            if step < self.line:
+                yield from self.from_z(phase, nearest(self.z, self.line, step))
+            for apart in range(1, self.wide):
+                if 0 <= step - apart < self.line:
+                    z_from = nearest(self.z, self.line, step - apart)
+                    yield from self.from_x(phase, z_from, nearest(self.x, self.wide, apart))
+            if 0 <= step - 1 < self.line and step > 1:
+                yield from self.from_plane(phase, nearest(self.z, self.line, step - 1), self.x, False)
+            for apart in range(1, self.wide):
+                if 0 <= step - apart - 1 < self.line:
+                    z_from = nearest(self.z, self.line, step - apart - 1)
+                    yield from self.from_plane(phase, z_from, nearest(self.x, self.wide, apart), True)
+
+    def from_z(self, phase, z_from):
+        at = (phase, self.core, z_from, self.x)
+        upward = z_from < self.z
+        onward = (upward & (self.z < self.line - 1)) | (~upward & (self.z > 0))
+        target = self.along_z(jnp.where(upward, 1, -1))
+        spans, cross = self.spans(False), self.spans(True)
+        for kind in (0, 1):
+            self.arrive(*at, kind, *spans[kind])
+            self.send(*at, kind, *spans[kind], target, onward)
+            self.over_x(at, kind, cross[kind])
+            if kind == 0:
+                self.send(*at, 2, *spans[kind], self.other_plane)
+            self.send(*at, kind, *spans[kind], self.other_core)
+            yield
+
+    def from_x(self, phase, z_from, x_from):
+        at = (phase, self.core, z_from, x_from)
+        cross = self.spans(True)
+        p = self.plane
+        upward = x_from < self.x
+        onward = (upward & (self.x < self.wide - 1)) | (~upward & (self.x > 0))
+        target = self.along_x(jnp.where(upward, 1, -1))
+        for kind in (0, 1):
+            self.arrive(*at, kind, *cross[kind])
+            if self.wide > 2:
+                self.send(*at, kind, *cross[kind], target, onward)
+            self.send(*at, kind + 2, *(cross[0] if kind == 0 else (4 + 3 * p, 1)), self.other_plane)
+            self.send(*at, kind, *cross[kind], self.other_core)
+            yield
+
+    def from_plane(self, phase, z_from, x_from, other):
+        at = (phase, self.core, z_from, x_from)
+        spans = self.spans(other)
+        for kind in range(2, len(spans)):
+            self.arrive(*at, kind, *spans[kind])
+            self.send(*at, kind, *spans[kind], self.other_core)
+        yield
+
+    def arrived(self, phase, z, x):
+        def pieces(other):
+            for kind, span in enumerate(self.spans(other)):
+                self.arrive(phase, 1 - self.core, z, x, kind, *span)
+
+        own_chip = (z == self.z) & (x == self.x)
+        same = (x == self.x) & (z != self.z)
+        pl.when(own_chip)(lambda: self.arrive(phase, 1 - self.core, z, x, 0, 0, 8))
+        pl.when(same)(lambda: pieces(False))
+        pl.when(x != self.x)(lambda: pieces(True))
+
+    def finish(self):
+        for copy, when in self.sends:
+            if when is None:
+                copy.wait_send()
+            else:
+                pl.when(when)(copy.wait_send)
+
+
+def sends_per_phase(count):
+    line = min(LINE, count // 2)
+    wide = count // (2 * line)
+    across = 1 if wide == 2 else 2
+    each = 2 * (2 + across) + 1
+    return line * each + (wide - 1) * line * 2 * (1 + across) + (line - 1) + (wide - 1) * line * 2
+
+
+def gather_kernel(count, self_qkv, self_out, cross_qkv, cross_out, ffn_in, ffn_out, attn, wide_in, wide_out, send_sem, recv_sem, own_sem):
+    index = lax.axis_index("fsdp")
+    thin = self_out.shape[0]
+    deep = ffn_out.shape[0]
+    unit = self_out.shape[1] // 8
+    unit_in = ffn_in.shape[1] // 8
+
+    def rows(start, many):
+        return pl.ds(pl.multiple_of(start * many, many), many)
+
+    def columns(first, units, width):
+        return pl.ds(pl.multiple_of(first * width, width), units * width)
+
+    views = (
+        lambda f, first, units: attn.at[pl.ds(0, 3), rows(f, thin), columns(first, units, unit)],
+        lambda f, first, units: attn.at[pl.ds(3, 5), rows(f, thin), columns(first, units, unit)],
+        lambda f, first, units: wide_in.at[rows(f, thin), columns(first, units, unit_in)],
+        lambda f, first, units: wide_out.at[rows(f, deep), columns(first, units, unit)],
+    )
+    mine = rows(index, thin)
+    owned = [
+        [(self_qkv, attn.at[pl.ds(0, 3), mine])],
+        [(self_out, attn.at[3, mine]), (cross_qkv, attn.at[pl.ds(4, 3), mine]), (cross_out, attn.at[7, mine])],
+        [(ffn_in, wide_in.at[mine])],
+        [(ffn_out, wide_out.at[rows(index, deep)])],
+    ]
+    copies = []
+    for group in owned:
+        copies.append([])
+        for one, to in group:
+            copy = pltpu.make_async_copy(one, to, own_sem.at[sum(map(len, copies))])
+            copy.start()
+            copies[-1].append(copy)
+    gather = Gather(count, views, send_sem, recv_sem)
+    gather.enter()
+
+    def begin(phase):
+        for copy in copies[phase]:
+            copy.wait()
+        gather.own(phase)
+
+    begin(0)
+    for phase in range(4):
+        if phase < 3:
+            begin(phase + 1)
+        for _ in gather.ticks(phase):
+            pass
+    for phase in range(4):
+        for z in range(gather.line):
+            for x in range(gather.wide):
+                gather.arrived(phase, z, x)
+    gather.finish()
+
+
+def gather_all(count, *parts):
+    line = min(LINE, count // 2)
+    return pl.pallas_call(
+        functools.partial(gather_kernel, count),
+        out_shape=[
+            jax.ShapeDtypeStruct((8, 1024, 1024), jnp.bfloat16),
+            jax.ShapeDtypeStruct((parts[4].shape[0] * count, parts[4].shape[1]), jnp.bfloat16),
+            jax.ShapeDtypeStruct((parts[5].shape[0] * count, parts[5].shape[1]), jnp.bfloat16),
+        ],
+        in_specs=[pl.BlockSpec(memory_space=pl.ANY)] * 6,
+        out_specs=[pl.BlockSpec(memory_space=pl.ANY)] * 3,
+        scratch_shapes=[
+            pltpu.SemaphoreType.DMA((4, sends_per_phase(count))),
+            pltpu.SemaphoreType.DMA((4, 2, count // 2, 4)),
+            pltpu.SemaphoreType.DMA((6,)),
+        ],
+        compiler_params=pltpu.CompilerParams(collective_id=0, has_side_effects=True),
+        name="gather_weights",
+    )(*parts)
 
 
 def local(
@@ -163,10 +427,10 @@
     branch_scale = step_value / (step_value + ramp_steps)
     self_mask = mask_maker(bucket_shift[0], seq_lengths[0], rows_here, True)
     cross_mask = mask_maker(bucket_shift[0], enc_lengths[0], rows_here, False)
-    self_whole, self_proj = (
-        lax.all_gather(self_qkv, "fsdp", axis=1, tiled=True),
-        lax.all_gather(self_out, "fsdp", axis=0, tiled=True),
-    )
+    attn_whole, ffn_whole_in, ffn_whole_out = gather_all(
+        lax.axis_size("fsdp"), self_qkv, self_out, cross_qkv, cross_out, ffn_in, ffn_out
+    )
+    self_whole, self_proj = attn_whole[:3], attn_whole[3]
     projected = jnp.einsum(
         "td,kde->kte", tokens, self_whole, preferred_element_type=jnp.float32
     ).astype(jnp.bfloat16)
@@ -178,10 +442,7 @@
     )
     first = normal_one * norm_gain[0] + norm_bias[0]
     first_low = first.astype(jnp.bfloat16)
-    cross_whole, cross_proj = (
-        lax.all_gather(cross_qkv, "fsdp", axis=1, tiled=True),
-        lax.all_gather(cross_out, "fsdp", axis=0, tiled=True),
-    )
+    cross_whole, cross_proj = attn_whole[4:7], attn_whole[7]
     cross_queries = jnp.dot(first_low, cross_whole[0], preferred_element_type=jnp.float32).astype(
         jnp.bfloat16
     )
@@ -195,10 +456,6 @@
     )
     second = normal_two * norm_gain[1] + norm_bias[1]
     second_low = second.astype(jnp.bfloat16)
-    ffn_whole_in, ffn_whole_out = (
-        lax.all_gather(ffn_in, "fsdp", axis=0, tiled=True),
-        lax.all_gather(ffn_out, "fsdp", axis=0, tiled=True),
-    )
     inner = jnp.dot(second_low, ffn_whole_in, preferred_element_type=jnp.float32)
     active = gelu_exact(inner).astype(jnp.bfloat16)
     narrow = jnp.dot(second_low, adapt_down, preferred_element_type=jnp.float32) + down_bias

time: 681 us -> 517 us (0.76)
  waiting for transfers between devices: 341 us -> 0.02 us
  Pallas kernels: 0 us -> 170 us
  matrix products: 212 us -> 219 us
    all_gather x6 -> x0, waiting for transfers between devices: 257 us -> none  [the longest x1 68.3 us: local(): lax.all_gather(ffn_in, 'fsdp', axis=0, tiled=True)]
    pallas_call x0 -> x1, Pallas kernels: none -> 170 us  [gather_all(): pl.pallas_call(functools.partial(gather_kernel, count), out_shape=[jax.Sh...]
    psum x1, waiting for transfers between devices: 80.2 us -> 0.01 us  [local(): lax.psum((grad_down, grad_downb, grad_up, grad_upb, gain_grads, bias_grad...]
  transfers between devices with their start and end apart: 7 -> 1, of which waited for: 7 -> 0; matrix products, arithmetic and copies ran while one was open for 18% -> 29% of each run, Pallas kernels for 0% -> 0%
where the time goes in v1:
time: 517 us; the launch traced here: 511 us
  matrix products  219 us (42%)
  Pallas kernels  170 us (33%)
  other arithmetic  46.2 us (9%)
  blocking collectives  39.7 us (8%)
  local copies, waits for them, and re-layouts  20.2 us (4%)
  between operations  16.3 us (3%)
    pallas_call x1, Pallas kernels, gather_all(): pl.pallas_call(functools.partial(gather_kernel, count), out_shape=[jax.Sh...  170 us
    psum x1, blocking collectives, local(): lax.psum((grad_down, grad_downb, grad_up, grad_upb, gain_grads, bias_grad...  39.7 us
    dot_general x2, matrix products, one_block(): jnp.einsum('thd,shd->hts', grad_heads, value_heads, preferred_element_typ...  28.7 us
    dot_general x1, matrix products, local(): jnp.dot(second_low, ffn_whole_in, preferred_element_type=jnp.float32)  23.2 us
    convert_element_type x2, other arithmetic, one_block(): grad_scores = (attn_probs * (grad_probs - row_delta)).astype(jnp.bfloat16)  21.6 us
    dot_general x1, matrix products, local(): jnp.einsum('tf,df->td', grad_inner, ffn_back_in, preferred_element_type=j...  19.3 us
    dot_general x2, matrix products, one_block(): jnp.einsum('hts,thd->shd', attn_probs.astype(jnp.bfloat16), grad_heads, p...  18.3 us
    reduce_sum x2, other arithmetic, one_block(): row_total = jnp.sum(expanded, -1, keepdims=True)  16.5 us
  transfers between devices with their start and end apart: 1, of which 0 were waited for; matrix products, arithmetic and copies ran while one was open for 29% of the time, Pallas kernels for 0%

profile of v1, /device:TPU:0, one launch (start us, length us, event | category | flops | bytes accessed | tf_op | source)
XLA Modules:
  0.0 511.0 jit_solution(3747991439104117135)
XLA Ops:
  12.0 170.0 %gather_weights.1 = (bf16[8,1024,1024]{2,1,0:T(8,128)(2,1)}, bf16[1024,4096]{1,0:T(8,128)(2,1)}, bf16[4096,1024]{1,0:T(8,128)(2,1)}) custom-call(bf16[3,64,1024]{2,1,0:T(8,128)(2,1)} %self_qkv.1, bf16[64,1024]{1,0:T(8,128)(2,1)} %self_out.1, bf16[3,64,1024]{2,1,0:T(8,128)(2,1)} %cross_qkv.1, bf16[64,1024]{1,0:T(8,128)(2,1)} %cross_out.1, ...), custom_call_target="tpu_custom_call" | custom-call | tf_op jit(solution)/shard_map/gather_weights/pallas_call | solution.py:386
  182.0 4.6 convert_bitcast_fusion.1
  187.8 7.4 %convert_bitcast_fusion = bf16[3,512,1024]{1,2,0:T(8,128)(2,1)S(1)} fusion(bf16[8,1024,1024]{2,1,0:T(8,128)(2,1)} %get-tuple-element.111, bf16[512,1024]{1,0:T(8,128)(2,1)S(1)} %copy-done.55), kind=kOutput, calls=%fused_computation.45 | convolution fusion | flops 3222798336 | bytes 20971520 | tf_op jit(solution)/shard_map/td,kde->kte/dot_general | solution.py:434
  196.1 7.4 %fusion.121 = (f32[16,512]{1,0:T(8,128)S(1)}, f32[16,512,512]{1,2,0:T(8,128)}) fusion(bf16[512,16,64]{0,2,1:T(8,128)(2,1)S(1)} %bitcast.170, bf16[512,16,64]{0,2,1:T(8,128)(2,1)S(1)} %bitcast.160, pred[512,512]{0,1:T(8,128)(4,1)S(1)} %get-tuple-element.188), kind=kOutput, calls=%fused_computation.183 | convolution fusion | flops 549445632 | bytes 19169280 | tf_op jit(solution)/shard_map/while/body/eval_jaxpr/thd,shd->hts/dot_general | solution.py:74
  203.5 8.3 %fusion = f32[16,512]{1,0:T(8,128)S(1)} fusion(f32[16,512,512]{1,2,0:T(8,128)} %get-tuple-element.190, f32[16,512]{1,0:T(8,128)S(1)} %get-tuple-element.189), kind=kLoop, calls=%fused_computation.12 | loop fusion | flops 8380416 | bytes 16842752 | tf_op jit(solution)/shard_map/while/body/eval_jaxpr/reduce_sum | solution.py:80
  211.8 7.6 %fusion.70 = bf16[16,64,512]{2,1,0:T(8,128)(2,1)S(1)} fusion(bf16[512,16,64]{0,2,1:T(8,128)(2,1)S(1)} %bitcast.172, f32[16,512,512]{1,2,0:T(8,128)} %get-tuple-element.190, f32[16,512]{1,0:T(8,128)S(1)} %fusion, f32[16,512]{1,0:T(8,128)S(1)} %get-tuple-element.189), kind=kOutput, calls=%fused_computation.121 | convolution fusion | flops 549978112 | bytes 18939904 | tf_op jit(solution)/shard_map/while/body/eval_jaxpr/hts,shd->thd/dot_general | solution.py:82
  223.7 3.9 fusion.74
  229.1 7.5 %fusion.123 = (f32[16,512]{1,0:T(8,128)S(1)}, f32[16,512,512]{1,2,0:T(8,128)}) fusion(bf16[512,16,64]{0,2,1:T(8,128)(2,1)S(1)} %bitcast.164, bf16[512,16,64]{0,2,1:T(8,128)(2,1)S(1)} %bitcast.162, pred[512,512]{0,1:T(8,128)(4,1)S(1)} %get-tuple-element.187), kind=kOutput, calls=%fused_computation.185 | convolution fusion | flops 549445632 | bytes 19169280 | tf_op jit(solution)/shard_map/while/body/eval_jaxpr/thd,shd->hts/dot_general | solution.py:74
  236.7 8.3 %fusion.1 = f32[16,512]{1,0:T(8,128)S(1)} fusion(f32[16,512,512]{1,2,0:T(8,128)} %get-tuple-element.194, f32[16,512]{1,0:T(8,128)S(1)} %get-tuple-element.193), kind=kLoop, calls=%fused_computation.13 | loop fusion | flops 8380416 | bytes 16842752 | tf_op jit(solution)/shard_map/while/body/eval_jaxpr/reduce_sum | solution.py:80
  245.0 7.7 %fusion.69 = bf16[16,64,512]{2,1,0:T(8,128)(2,1)S(1)} fusion(bf16[512,16,64]{0,2,1:T(8,128)(2,1)S(1)} %bitcast.174, f32[16,512,512]{1,2,0:T(8,128)} %get-tuple-element.194, f32[16,512]{1,0:T(8,128)S(1)} %fusion.1, f32[16,512]{1,0:T(8,128)S(1)} %get-tuple-element.193), kind=kOutput, calls=%fused_computation.120 | convolution fusion | flops 549978112 | bytes 18939904 | tf_op jit(solution)/shard_map/while/body/eval_jaxpr/hts,shd->thd/dot_general | solution.py:82
  252.7 3.2 fusion.124
  256.8 23.2 %fusion.4 = (f32[512,4096]{1,0:T(8,128)S(1)}, f32[512,4096]{1,0:T(8,128)}) fusion(bf16[512,1024]{1,0:T(8,128)(2,1)S(1)} %fusion.57, bf16[1024,4096]{1,0:T(8,128)(2,1)S(1)} %bitcast.208), kind=kOutput, calls=%fused_computation.17 | convolution fusion | flops 4424990720 | bytes 26214400 | tf_op jit(solution)/shard_map/dot_general | solution.py:459
  280.8 11.7 %fusion.18 = f32[512,1024]{1,0:T(8,128)} fusion(bf16[4096,1024]{1,0:T(8,128)(2,1)S(1)} %bitcast.210, f32[512,4096]{1,0:T(8,128)S(1)} %get-tuple-element.197, f32[512,4096]{1,0:T(8,128)} %get-tuple-element.198), kind=kOutput, calls=%fused_computation.39 | convolution fusion | flops 4301258752 | bytes 27262976 | tf_op jit(solution)/shard_map/dot_general | solution.py:466
  306.4 19.3 %fusion.20 = f32[512,1024]{1,0:T(8,128)} fusion(bf16[1024,4096]{1,0:T(8,128)(2,1)} %get-tuple-element.112, f32[512,4096]{1,0:T(8,128)} %copy-done.64, f32[512,4096]{1,0:T(8,128)} %get-tuple-element.198, bf16[4096,1024]{1,0:T(8,128)(2,1)} %get-tuple-element.113, f32[512,1024]{1,0:T(8,128)} %copy-done.14), kind=kOutput, calls=%fused_computation.41 | convolution fusion | flops 8619819008 | bytes 37748736 | tf_op jit(solution)/shard_map/tf,df->td/dot_general | solution.py:489
  325.7 4.5 multiply_reduce_fusion.2
  331.5 4.1 fusion.77
  337.2 9.7 %fusion.80 = bf16[16,64,512]{2,1,0:T(8,128)(2,1)} fusion(bf16[512,16,64]{0,2,1:T(8,128)(2,1)S(1)} %bitcast.168, f32[16,512,512]{1,2,0:T(8,128)} %get-tuple-element.194, f32[16,512]{1,0:T(8,128)S(1)} %log_add_fusion.1), kind=kOutput, calls=%fused_computation.125 | convolution fusion | flops 545783808 | bytes 18907136 | tf_op jit(solution)/shard_map/while/body/eval_jaxpr/hts,thd->shd/dot_general | solution.py:125
  346.9 14.0 %multiply_reduce_fusion.1 = (f32[16,512]{1,0:T(8,128)}, f32[16,512,512]{1,2,0:T(8,128)}) fusion(f32[16,512,512]{1,2,0:T(8,128)} %get-tuple-element.194, f32[16,512]{1,0:T(8,128)} %copy-done.31, bf16[512,16,64]{0,2,1:T(8,128)(2,1)S(1)} %bitcast.169, bf16[512,16,64]{0,2,1:T(8,128)(2,1)} %bitcast.175), kind=kOutput, calls=%fused_computation.4 | convolution fusion | flops 549445632 | bytes 35717120 | tf_op jit(solution)/shard_map/while/body/eval_jaxpr/thd,shd->hts/dot_general | solution.py:109
  360.9 10.9 %multiply_convert_fusion.1 = bf16[16,512,512]{1,2,0:T(8,128)(2,1)} fusion(f32[16,512,512]{1,2,0:T(8,128)} %get-tuple-element.203, f32[16,512,512]{1,2,0:T(8,128)S(1)} %bitcast.159, f32[16,512]{1,0:T(8,128)} %get-tuple-element.202, f32[16,512]{1,0:T(8,128)} %copy-done.31), kind=kLoop, calls=%fused_computation.3 | loop fusion | flops 16777216 | bytes 42008576 | tf_op jit(solution)/shard_map/while/body/eval_jaxpr/convert_element_type | solution.py:113
  371.8 7.5 %multiply_convert_fusion.4 = bf16[16,64,512]{2,1,0:T(8,128)(2,1)} fusion(bf16[512,16,64]{0,2,1:T(8,128)(2,1)} %bitcast.165, bf16[16,512,512]{1,2,0:T(8,128)(2,1)} %multiply_convert_fusion.1), kind=kOutput, calls=%fused_computation.81 | convolution fusion | flops 537919488 | bytes 10485760 | tf_op jit(solution)/shard_map/while/body/eval_jaxpr/hts,thd->shd/dot_general | solution.py:120
  382.3 4.8 multiply_reduce_fusion.3
  392.1 14.7 %multiply_reduce_fusion = (f32[16,512]{1,0:T(8,128)}, f32[16,512,512]{1,2,0:T(8,128)}) fusion(f32[16,512,512]{1,2,0:T(8,128)} %get-tuple-element.190, f32[16,512]{1,0:T(8,128)} %log_add_fusion, bf16[512,16,64]{0,2,1:T(8,128)(2,1)S(1)} %bitcast.166, bf16[512,16,64]{0,2,1:T(8,128)(2,1)} %bitcast.173), kind=kOutput, calls=%fused_computation.1 | convolution fusion | flops 549445632 | bytes 35717120 | tf_op jit(solution)/shard_map/while/body/eval_jaxpr/thd,shd->hts/dot_general | solution.py:109
  409.3 10.8 %multiply_convert_fusion = bf16[16,512,512]{1,2,0:T(8,128)(2,1)} fusion(f32[16,512,512]{1,2,0:T(8,128)} %get-tuple-element.206, f32[16,512,512]{1,2,0:T(8,128)S(1)} %bitcast.157, f32[16,512]{1,0:T(8,128)} %get-tuple-element.205, f32[16,512]{1,0:T(8,128)} %log_add_fusion), kind=kLoop, calls=%fused_computation | loop fusion | flops 16777216 | bytes 42008576 | tf_op jit(solution)/shard_map/while/body/eval_jaxpr/convert_element_type | solution.py:113
  420.1 6.8 %multiply_convert_fusion.5 = bf16[16,64,512]{2,1,0:T(8,128)(2,1)S(1)} fusion(bf16[512,16,64]{0,2,1:T(8,128)(2,1)} %bitcast.171, bf16[16,512,512]{1,2,0:T(8,128)(2,1)} %multiply_convert_fusion), kind=kOutput, calls=%fused_computation.85 | convolution fusion | flops 537919488 | bytes 10485760 | tf_op jit(solution)/shard_map/while/body/eval_jaxpr/hts,thd->shd/dot_general | solution.py:120
  428.4 4.2 fusion.28
  432.7 4.3 fusion.34
  437.0 4.3 fusion.36
  441.4 39.7 %all-reduce = (f32[512]{0:T(512)}, f32[1024]{0:T(1024)}, f32[3,1024]{1,0:T(4,128)}, f32[3,1024]{1,0:T(4,128)}) all-reduce(f32[512]{0:T(512)S(1)} %copy-done.47, f32[1024]{0:T(1024)S(1)} %copy-done.37, f32[3,1024]{1,0:T(4,128)S(1)} %pad_maximum_fusion, ...), channel_id=1, replica_groups=mesh['fsdp'=16,'dp'=2] {'fsdp','dp'}, use_global_device_ids=true, to_apply=%region_22.23 | all-reduce | flops 7680 | bytes 61440 | tf_op jit(solution)/shard_map/psum | solution.py:533
  481.1 4.6 add_convert_fusion.2
  485.8 8.6 %fusion.83 = bf16[16,64,512]{2,1,0:T(8,128)(2,1)S(1)} fusion(bf16[512,16,64]{0,2,1:T(8,128)(2,1)S(1)} %bitcast.167, f32[16,512,512]{1,2,0:T(8,128)} %get-tuple-element.190, f32[16,512]{1,0:T(8,128)S(1)} %copy-done.30), kind=kOutput, calls=%fused_computation.126 | convolution fusion | flops 545783808 | bytes 18907136 | tf_op jit(solution)/shard_map/while/body/eval_jaxpr/hts,thd->shd/dot_general | solution.py:125
  494.5 4.6 add_convert_fusion.3
  499.1 3.2 copy.82
  (205 shorter events, 43.4 us)
Async XLA Ops:
  7.2 174.8 %copy-start = (bf16[512,1024]{1,0:T(8,128)(2,1)S(1)}, bf16[512,1024]{1,0:T(8,128)(2,1)}, u32[]{:S(2)}) copy-start(bf16[512,1024]{1,0:T(8,128)(2,1)} %param.19) | copy-start | bytes 3145732
  7.2 491.9 %all-reduce.4.cloned.1.call-start = ((), (), s32[]{:S(2)}) async-start(), calls=%async_computation | async-start | bytes 8388608 | tf_op jit(solution)/shard_map/psum | solution.py:533
  10.6 242.1 %copy-start.44 = (f32[1,1024]{1,0:T(1,128)}, f32[1,1024]{1,0:T(1,128)S(1)}, u32[]{:S(2)}) copy-start(f32[1,1024]{1,0:T(1,128)S(1)} %get-tuple-element.169) | copy-start | bytes 12292
  187.8 41.3 %copy-start.8 = (bf16[1,512,1024]{1,2,0:T(8,128)(2,1)}, bf16[1,512,1024]{1,2,0:T(8,128)(2,1)S(1)}, u32[]{:S(2)}) copy-start(bf16[1,512,1024]{1,2,0:T(8,128)(2,1)S(1)} %get-tuple-element.166) | copy-start | bytes 3145732
  187.8 57.2 %copy-start.16 = (bf16[1,512,1024]{1,2,0:T(8,128)(2,1)}, bf16[1,512,1024]{1,2,0:T(8,128)(2,1)S(1)}, u32[]{:S(2)}) copy-start(bf16[1,512,1024]{1,2,0:T(8,128)(2,1)S(1)} %get-tuple-element.167) | copy-start | bytes 3145732
  195.4 16.4 %copy-start.15 = (bf16[1,512,1024]{1,2,0:T(8,128)(2,1)}, bf16[1,512,1024]{1,2,0:T(8,128)(2,1)S(1)}, u32[]{:S(2)}) copy-start(bf16[1,512,1024]{1,2,0:T(8,128)(2,1)S(1)} %get-tuple-element.164) | copy-start | bytes 3145732
  222.4 30.3 %copy-start.39 = (f32[512]{0:T(512)}, f32[512]{0:T(512)S(1)}, u32[]{:S(2)}) copy-start(f32[512]{0:T(512)S(1)} %broadcast_multiply_fusion.8) | copy-start | bytes 6148
  222.8 29.9 %copy-start.48 = (f32[512]{0:T(512)}, f32[512]{0:T(512)S(1)}, u32[]{:S(2)}) copy-start(f32[512]{0:T(512)S(1)} %add_rsqrt_fusion.2) | copy-start | bytes 6148
  255.9 74.3 %copy-start.4 = (f32[512,1024]{1,0:T(8,128)}, f32[512,1024]{1,0:T(8,128)S(1)}, u32[]{:S(2)}) copy-start(f32[512,1024]{1,0:T(8,128)S(1)} %get-tuple-element.196) | copy-start | bytes 6291460
  255.9 24.8 %slice-start.10 = ((s8[8388608]{0:T(1024)(128)(4,1)}), s8[4194304]{0:T(1024)(128)(4,1)S(1)}, s32[]{:S(2)}) async-start(s8[8388608]{0:T(1024)(128)(4,1)} %bitcast.209), calls=%async_computation.11 | async-start | bytes 8388608
  256.8 23.2 %copy-start.27 = (bf16[1024,512]{1,0:T(8,128)(2,1)S(1)}, bf16[1024,512]{1,0:T(8,128)(2,1)}, u32[]{:S(2)}) copy-start(bf16[1024,512]{1,0:T(8,128)(2,1)} %param.27) | copy-start | bytes 3145732
  256.8 23.2 %copy-start.59 = (f32[512]{0:T(512)S(1)}, f32[512]{0:T(512)}, u32[]{:S(2)}) copy-start(f32[512]{0:T(512)} %param.28) | copy-start | bytes 6148
  256.8 24.0 %slice-start.11 = ((s8[8388608]{0:T(1024)(128)(4,1)}), s8[4194304]{0:T(1024)(128)(4,1)S(1)}, s32[]{:S(2)}) async-start(s8[8388608]{0:T(1024)(128)(4,1)} %bitcast.209), calls=%async_computation.12 | async-start | bytes 8388608
  280.0 12.5 %copy-start.64 = (f32[512,4096]{1,0:T(8,128)}, f32[512,4096]{1,0:T(8,128)S(1)}, u32[]{:S(2)}) copy-start(f32[512,4096]{1,0:T(8,128)S(1)} %get-tuple-element.197) | copy-start | bytes 25165828
  280.8 11.7 %copy-start.57 = (bf16[512,1024]{1,0:T(8,128)(2,1)S(1)}, bf16[512,1024]{1,0:T(8,128)(2,1)}, u32[]{:S(2)}) copy-start(bf16[512,1024]{1,0:T(8,128)(2,1)} %param.29) | copy-start | bytes 3145732
  280.8 11.7 %copy-start.58 = (f32[1024]{0:T(1024)S(1)}, f32[1024]{0:T(1024)}, u32[]{:S(2)}) copy-start(f32[1024]{0:T(1024)} %param.30) | copy-start | bytes 12292
  306.3 30.8 %copy-start.31 = (f32[16,512]{1,0:T(8,128)}, f32[16,512]{1,0:T(8,128)S(1)}, u32[]{:S(2)}) copy-start(f32[16,512]{1,0:T(8,128)S(1)} %log_add_fusion.1) | copy-start | bytes 98308
  306.4 19.4 %copy-start.19 = (bf16[512,512]{1,0:T(8,128)(2,1)S(1)}, bf16[512,512]{1,0:T(8,128)(2,1)}, u32[]{:S(2)}) copy-start(bf16[512,512]{1,0:T(8,128)(2,1)} %copy-done.18) | copy-start | bytes 1572868
  337.2 23.7 %slice-start.4 = ((s8[16777216]{0:T(1024)(128)(4,1)}), s8[4194304]{0:T(1024)(128)(4,1)S(1)}, s32[]{:S(2)}) async-start(s8[16777216]{0:T(1024)(128)(4,1)} %bitcast.158), calls=%async_computation.5 | async-start | bytes 8388608
  337.2 23.7 %slice-start.5 = ((s8[16777216]{0:T(1024)(128)(4,1)}), s8[4194304]{0:T(1024)(128)(4,1)S(1)}, s32[]{:S(2)}) async-start(s8[16777216]{0:T(1024)(128)(4,1)} %bitcast.158), calls=%async_computation.6 | async-start | bytes 8388608
  346.9 14.0 %slice-start.6 = ((s8[16777216]{0:T(1024)(128)(4,1)}), s8[4194304]{0:T(1024)(128)(4,1)S(1)}, s32[]{:S(2)}) async-start(s8[16777216]{0:T(1024)(128)(4,1)} %bitcast.158), calls=%async_computation.7 | async-start | bytes 8388608
  346.9 14.0 %slice-start.7 = ((s8[16777216]{0:T(1024)(128)(4,1)}), s8[4194304]{0:T(1024)(128)(4,1)S(1)}, s32[]{:S(2)}) async-start(s8[16777216]{0:T(1024)(128)(4,1)} %bitcast.158), calls=%async_computation.8 | async-start | bytes 8388608
  392.1 14.8 %copy-start.11 = (bf16[512,1024]{0,1:T(8,128)(2,1)}, bf16[512,1024]{0,1:T(8,128)(2,1)S(1)}, u32[]{:S(2)}) copy-start(bf16[512,1024]{0,1:T(8,128)(2,1)S(1)} %copy.63) | copy-start | bytes 3145732
  392.1 14.8 %slice-start = ((s8[16777216]{0:T(1024)(128)(4,1)}), s8[4194304]{0:T(1024)(128)(4,1)S(1)}, s32[]{:S(2)}) async-start(s8[16777216]{0:T(1024)(128)(4,1)} %bitcast.156), calls=%async_computation.1 | async-start | bytes 8388608
  392.1 14.8 %slice-start.1 = ((s8[16777216]{0:T(1024)(128)(4,1)}), s8[4194304]{0:T(1024)(128)(4,1)S(1)}, s32[]{:S(2)}) async-start(s8[16777216]{0:T(1024)(128)(4,1)} %bitcast.156), calls=%async_computation.2 | async-start | bytes 8388608
  392.1 16.0 %slice-start.2 = ((s8[16777216]{0:T(1024)(128)(4,1)}), s8[4194304]{0:T(1024)(128)(4,1)S(1)}, s32[]{:S(2)}) async-start(s8[16777216]{0:T(1024)(128)(4,1)} %bitcast.156), calls=%async_computation.3 | async-start | bytes 8388608
  392.1 17.2 %slice-start.3 = ((s8[16777216]{0:T(1024)(128)(4,1)}), s8[4194304]{0:T(1024)(128)(4,1)S(1)}, s32[]{:S(2)}) async-start(s8[16777216]{0:T(1024)(128)(4,1)} %bitcast.156), calls=%async_computation.4 | async-start | bytes 8388608
  437.0 44.1 %copy-start.28 = (bf16[16,64,512]{2,1,0:T(8,128)(2,1)S(1)}, bf16[16,64,512]{2,1,0:T(8,128)(2,1)}, u32[]{:S(2)}) copy-start(bf16[16,64,512]{2,1,0:T(8,128)(2,1)} %multiply_convert_fusion.4) | copy-start | bytes 3145732
  485.7 8.7 %copy-start.41 = (f32[512]{0:T(512)S(1)}, f32[512]{0:T(512)}, u32[]{:S(2)}) copy-start(f32[512]{0:T(512)} %copy-done.39) | copy-start | bytes 6148
  485.7 8.7 %copy-start.46 = (f32[1,1024]{1,0:T(1,128)S(1)}, f32[1,1024]{1,0:T(1,128)}, u32[]{:S(2)}) copy-start(f32[1,1024]{1,0:T(1,128)} %copy-done.44) | copy-start | bytes 12292
  485.7 8.7 %copy-start.50 = (f32[512]{0:T(512)S(1)}, f32[512]{0:T(512)}, u32[]{:S(2)}) copy-start(f32[512]{0:T(512)} %copy-done.48) | copy-start | bytes 6148
  485.7 8.7 %copy-start.61 = (f32[512,1024]{1,0:T(8,128)S(1)}, f32[512,1024]{1,0:T(8,128)}, u32[]{:S(2)}) copy-start(f32[512,1024]{1,0:T(8,128)} %copy-done.60) | copy-start | bytes 6291460
  (46 other events, 205.3 us)
Sparse Core Ops, SparseCore 0:
  305.8 141.8 all-reduce.3
